TPU v7x, 256 devices: a whole 4x4x8 slice. The times are simulated.
256 devices in a mesh: particle: 16 (over x, y_lo, core), shard: 16 (over z, y_hi).
Axes of the slice: x: 4, y: 4 (y_hi: 2, y_lo: 2; y = y_hi * 2 + y_lo), z: 8, core: 2. Of those that a mesh axis runs over, the one named last changes fastest.
Arguments:
- pool: bfloat16 [16384, 1024], P('shard'), may hold values from -6 to 6
- batch_index: int32 [8192], P('shard'), may hold values from 0 to 1023
- kernel_scale: int32 [1], replicated, may hold values from 4194304 to 8388607
- cotangent: bfloat16 [16, 8192, 1024], P('particle', 'shard'), may hold values from -6 to 6
- weights: float32 [16, 1024, 2, 2048], P('particle', 'shard'), may hold values from -10 to 10
- first_moment: float32 [16, 1024, 2, 2048], P('particle', 'shard'), may hold values from -2 to 2
- second_moment: float32 [16, 1024, 2, 2048], P('particle', 'shard'), may hold values from 0.01 to 1
Outputs:
- new_weights: float32 [16, 1024, 2, 2048], P('particle', 'shard')
- new_first: float32 [16, 1024, 2, 2048], P('particle', 'shard')
- new_second: float32 [16, 1024, 2, 2048], P('particle', 'shard')
- transport: float32 [16, 1024, 2, 2048], P('particle', 'shard')
Inputs may be any that keep to these rules, and one draw needn't show every extreme that they name: `batch_index`: each entry names a row of the pool block that the same index of shard holds.
All inputs are finite; a program needn't handle non-finite values.
Results may differ from a plain program's by a relative error of at most 0.015.
Values may be sent and summed in bfloat16 or wider, within the bound.
A program may use at most 192 MiB of HBM per device.

v0:
```python
import jax
import jax.numpy as jnp
from jax import lax
from jax.sharding import PartitionSpec as P


def gelu_pair(up_proj):
    cdf_part = 0.5 * (1.0 + jax.scipy.special.erf(up_proj * 0.7071067811865476))
    density = jnp.exp(-0.5 * up_proj * up_proj) * 0.3989422804014327
    return (up_proj * cdf_part, cdf_part + up_proj * density)


def local(pool, batch_index, kernel_scale, cotangent, weights, first_moment, second_moment):
    shard_count = lax.axis_size("shard")
    particles = lax.axis_size("particle")
    tok_rows = batch_index.shape[0]
    model_width = pool.shape[1]
    hidden_units = weights.shape[3]
    picked = jnp.take(pool, batch_index, axis=0).astype(jnp.float32)
    normed = (picked * lax.rsqrt(jnp.mean(picked * picked, axis=1, keepdims=True) + 1e-06)).astype(
        jnp.bfloat16
    )
    upstream = cotangent[0]
    local_b = weights[0].astype(jnp.bfloat16)
    block_rows = lax.all_gather(local_b, "shard", axis=0, tiled=True)
    left_cols = normed
    right_cols = upstream
    up_part = jnp.dot(left_cols, block_rows[:, 0, :], preferred_element_type=jnp.float32)
    back_part = jnp.dot(right_cols, block_rows[:, 1, :], preferred_element_type=jnp.float32)
    up_proj = up_part * model_width ** (-0.5)
    back_proj = back_part * hidden_units ** (-0.5)
    act_full, gelu_slope = gelu_pair(up_proj)
    activation = act_full.astype(jnp.bfloat16)
    up_grad = (back_proj * gelu_slope).astype(jnp.bfloat16)
    grad_scale = 1.0 / (tok_rows * shard_count * model_width)
    contract = (((0,), (0,)), ((), ()))
    left_cols = normed
    right_cols = upstream
    g_up = lax.dot_general(left_cols, up_grad, contract, preferred_element_type=jnp.float32)
    g_down = lax.dot_general(right_cols, activation, contract, preferred_element_type=jnp.float32)
    g_up = g_up * (model_width ** (-0.5) * grad_scale)
    g_down = g_down * (hidden_units ** (-0.5) * grad_scale)
    grad_sum = lax.psum_scatter(
        jnp.stack([g_up, g_down], axis=1).astype(jnp.bfloat16),
        "shard",
        scatter_dimension=0,
        tiled=True,
    ).astype(jnp.float32)
    score_b = (-grad_sum).astype(jnp.bfloat16)
    inverse_band = 1.0 / kernel_scale[0].astype(jnp.float32)
    repulse = 2.0 * inverse_band
    own_w = lax.optimization_barrier(local_b).astype(jnp.float32)
    all_w, all_scores = (
        lax.all_gather(local_b[None], "particle", axis=0, tiled=True),
        lax.all_gather(score_b[None], "particle", axis=0, tiled=True),
    )
    all_wf = all_w.astype(jnp.float32)
    offset_sq = own_w[None] - all_wf
    partial_row = jnp.sum(offset_sq * offset_sq, axis=(1, 2, 3))
    distances = lax.psum(partial_row, "shard")
    kernel = jnp.exp(-distances * inverse_band)
    kernel_total = jnp.sum(kernel)
    pushed_field = all_scores.astype(jnp.float32) - repulse * all_wf
    term_rows = (kernel[:, None, None, None] * pushed_field).astype(jnp.bfloat16)
    weighted = jnp.sum(lax.optimization_barrier(term_rows).astype(jnp.float32), axis=0)
    params_total = 2 * model_width * hidden_units
    transport = params_total / particles * (weighted + repulse * kernel_total * own_w)
    new_first = 0.9 * first_moment[0] - 0.1 * transport
    new_second = 0.999 * second_moment[0] + 0.001 * transport * transport
    new_weights = weights[0] - 0.01 * new_first / (jnp.sqrt(new_second) + 1e-08)
    return (new_weights[None], new_first[None], new_second[None], transport[None])


def solution(mesh):
    placed = (
        P("shard", None),
        P("shard"),
        P(),
        P("particle", "shard", None),
        P("particle", "shard", None, None),
        P("particle", "shard", None, None),
        P("particle", "shard", None, None),
    )
    return jax.shard_map(
        local,
        mesh=mesh,
        in_specs=placed,
        out_specs=(
            P("particle", "shard", None, None),
            P("particle", "shard", None, None),
            P("particle", "shard", None, None),
            P("particle", "shard", None, None),
        ),
        check_vma=False,
    )
```

profile of v0, /device:TPU:1, one launch (start us, length us, event | category | flops | bytes accessed | tf_op | source)
XLA Modules:
  0.0 503.9 jit_solution(2273082299362088722)
XLA Ops:
  8.0 0.0 copy-start
  8.0 0.0 all-gather.7.cloned.1.call-start
  8.1 2.6 bitcast_convert_fusion
  10.6 0.0 all-gather.7.cloned.1.call-update
  10.6 0.0 reduce-scatter.2.cloned.1.call-start
  10.7 0.7 compare_select_fusion
  11.4 0.0 copy-done
  11.4 0.0 copy-start.7
  11.4 2.1 gather_fusion
  13.5 0.0 copy-done.7
  13.5 0.4 fusion.9
  13.9 137.3 %all-gather.7.cloned.1.call-done = bf16[1024,2,2048]{2,1,0:T(2,128)(2,1)} async-done(((bf16[64,2,2048]{2,1,0:T(2,128)(2,1)}), bf16[1024,2,2048]{2,1,0:T(2,128)(2,1)}) %all-gather.7.cloned.1.call-update) | async-done | bytes 8388624 | tf_op jit(solution)/shard_map/all_gather | solution.py:25
  151.3 17.1 %fusion.27 = (bf16[1024,1,2048]{2,1,0:T(2,128)(2,1)}, bf16[1024,1,2048]{2,1,0:T(2,128)(2,1)S(1)}) fusion(bf16[1024,2,2048]{2,1,0:T(2,128)(2,1)} %all-gather.7.cloned.1.call-done), kind=kLoop, calls=%fused_computation.51 | loop fusion | bytes 16777216 | tf_op jit(solution)/shard_map/slice | solution.py:29
  168.4 0.0 copy-start.8
  168.4 3.1 fusion.5
  171.6 0.0 copy-done.8
  171.6 0.0 copy-start.9
  171.6 4.2 fusion.8
  175.7 0.0 copy-done.9
  175.7 11.7 %fusion.7 = bf16[1024,1,2048]{2,0,1:T(8,128)(2,1)} fusion(f32[512,2048]{1,0:T(8,128)} %copy-done.9, bf16[1024,1,2048]{2,1,0:T(2,128)(2,1)} %get-tuple-element.10, bf16[1,512,1024]{2,1,0:T(8,128)(2,1)S(1)} %copy-done.8, f32[512]{0:T(512)S(1)} %add_rsqrt_fusion, bf16[512,1024]{1,0:T(8,128)(2,1)S(1)} %gather_fusion, pred[512]{0:T(512)(128)(4,1)S(1)} %compare_and_fusion), kind=kOutput, calls=%fused_computation.19 | convolution fusion | flops 4313841664 | bytes 14682624 | tf_op jit(solution)/shard_map/dot_general | solution.py:39
  187.4 7.5 %pad_maximum_fusion = bf16[1024,2,2048]{2,0,1:T(8,128)(2,1)} fusion(bf16[1024,1,2048]{2,0,1:T(8,128)(2,1)} %fusion.8, bf16[1024,1,2048]{2,0,1:T(8,128)(2,1)} %fusion.7), kind=kLoop, calls=%fused_computation.9 | loop fusion | flops 4194304 | bytes 16777216 | tf_op jit(solution)/shard_map/stack | solution.py:44
  194.9 0.0 copy-start.2
  194.9 0.0 copy-start.3
  194.9 0.0 reduce-scatter.2.cloned.1.call-update
  194.9 0.2 all-gather.5.cloned.1.call-start
  195.1 1.0 copy-done.2
  196.1 1.4 copy.58
  197.5 0.0 all-gather.5.cloned.1.call-update
  197.5 0.0 all-gather.9.cloned.1.call-start
  197.5 221.5 %reduce-scatter.2.cloned.1.call-done = bf16[64,2,2048]{2,0,1:T(8,128)(2,1)} async-done(((bf16[1024,2,2048]{2,0,1:T(8,128)(2,1)}), bf16[64,2,2048]{2,0,1:T(8,128)(2,1)}) %reduce-scatter.2.cloned.1.call-update) | async-done | bytes 524304 | tf_op jit(solution)/shard_map/reduce_scatter | solution.py:43
  419.0 1.9 negate_convert_fusion
  421.0 0.0 all-gather.9.cloned.1.call-update
  421.0 0.0 copy-done.3
  421.0 0.2 copy.28
  421.9 0.0 all-gather.5.cloned.1.call-done
  421.9 5.7 %fusion.1 = f32[16]{0:T(128)S(1)} fusion(bf16[16,64,2,2048]{3,1,2,0:T(8,128)(2,1)} %all-gather.5.cloned.1.call-done, f32[64,2,2048]{2,0,1:T(8,128)S(1)} %copy.28), kind=kLoop, calls=%fused_computation.4 | loop fusion | flops 16777200 | bytes 9437248 | tf_op jit(solution)/shard_map/reduce_sum | solution.py:59
  427.6 31.4 %psum.7 = f32[16]{0:T(128)S(1)} all-reduce(f32[16]{0:T(128)S(1)} %fusion.1), channel_id=1, replica_groups=mesh['particle'=16,'shard'=16] {'shard'}, use_global_device_ids=true, to_apply=%region_1.2 | all-reduce | flops 16 | bytes 128 | tf_op jit(solution)/shard_map/psum | solution.py:60
  459.0 0.6 fusion.26
  460.3 19.6 %all-gather.9.cloned.1.call-done = bf16[1024,2,2048]{2,0,1:T(8,128)(2,1)} async-done(((bf16[64,2,2048]{2,0,1:T(8,128)(2,1)}), bf16[1024,2,2048]{2,0,1:T(8,128)(2,1)}) %all-gather.9.cloned.1.call-update) | async-done | bytes 8388624 | tf_op jit(solution)/shard_map/all_gather | solution.py:55
  479.9 7.9 %fusion.4 = bf16[16,64,2,2048]{3,1,2,0:T(8,128)(2,1)S(1)} fusion(bf16[16,64,2,2048]{3,1,2,0:T(8,128)(2,1)} %all-gather.5.cloned.1.call-done, f32[]{:T(128)S(6)} %mul_shard_map.3, f32[16]{0:T(128)S(1)} %get-tuple-element.9, bf16[16,64,2,2048]{3,1,0,2:T(8,128)(2,1)} %bitcast.51), kind=kLoop, calls=%fused_computation.7 | loop fusion | flops 25165824 | bytes 25165892 | tf_op jit(solution)/shard_map/convert_element_type | solution.py:64
  487.7 0.0 copy-start.4
  487.7 0.0 copy-start.5
  487.8 0.0 copy-start.6
  487.8 0.0 copy-start.1
  487.8 1.9 convert_reduce_fusion
  489.7 0.0 copy-done.4
  489.7 0.0 copy-done.5
  489.7 0.0 copy-done.6
  489.7 6.8 %fusion.25 = (f32[1,64,2,2048]{3,2,1,0:T(2,128)}, f32[1,64,2,2048]{3,2,1,0:T(2,128)}, f32[1,64,2,2048]{3,2,1,0:T(2,128)}, f32[1,64,2,2048]{3,2,1,0:T(2,128)}) fusion(f32[1,64,2,2048]{3,2,1,0:T(2,128)S(1)} %copy-done.5, bf16[64,2,2048]{2,1,0:T(2,128)(2,1)S(1)} %copy-done.4, f32[]{:T(128)S(6)} %mul.182, f32[64,2,2048]{2,0,1:T(8,128)S(1)} %convert_reduce_fusion, ...), kind=kLoop, calls=%fused_computation.49 | loop fusion | flops 3932160 | bytes 8912900 | tf_op jit(solution)/shard_map/broadcast_in_dim | solution.py:71
  496.5 0.0 copy-done.1
  (3 shorter events, 0.0 us)
Async XLA Ops:
  8.0 3.4 copy-start
  8.0 143.3 %all-gather.7.cloned.1.call-start = ((), (), s32[]{:S(2)}) async-start(), calls=%async_computation.2 | async-start | bytes 8912896 | tf_op jit(solution)/shard_map/all_gather | solution.py:25
  10.6 408.4 %reduce-scatter.2.cloned.1.call-start = ((), (), s32[]{:S(2)}) async-start(), calls=%async_computation.3 | async-start | bytes 8912896 | tf_op jit(solution)/shard_map/reduce_scatter | solution.py:43
  11.4 2.1 copy-start.7
  168.4 3.1 copy-start.8
  171.6 4.2 copy-start.9
  194.9 1.2 copy-start.2
  194.9 226.1 %copy-start.3 = (bf16[64,2,2048]{2,1,0:T(2,128)(2,1)S(1)}, bf16[64,2,2048]{2,1,0:T(2,128)(2,1)}, u32[]{:S(2)}) copy-start(bf16[64,2,2048]{2,1,0:T(2,128)(2,1)} %bitcast_convert_fusion) | copy-start | bytes 1572868
  194.9 227.0 %all-gather.5.cloned.1.call-start = ((), (), s32[]{:S(2)}) async-start(), calls=%async_computation.1 | async-start | bytes 8912896 | tf_op jit(solution)/shard_map/all_gather | solution.py:54
  197.5 282.4 %all-gather.9.cloned.1.call-start = ((), (), s32[]{:S(2)}) async-start(), calls=%async_computation.4 | async-start | bytes 8912896 | tf_op jit(solution)/shard_map/all_gather | solution.py:55
  487.7 1.9 copy-start.4
  487.7 1.9 copy-start.5
  487.8 1.9 copy-start.6
  487.8 8.7 %copy-start.1 = (bf16[1024,1024]{1,0:T(8,128)(2,1)S(1)}, bf16[1024,1024]{1,0:T(8,128)(2,1)}, u32[]{:S(2)}) copy-start(bf16[1024,1024]{1,0:T(8,128)(2,1)} %param.7) | copy-start | bytes 6291460
Sparse Core Ops, SparseCore 0:
  12.0 139.2 all-gather.6
  195.0 223.9 reduce-scatter.1
Sparse Core Ops, SparseCore 1:
  197.8 60.7 all-gather.4
  421.1 58.7 all-gather.8
where the time goes:
time: 504 us
  waiting for transfers between devices  379 us (75%)
  other arithmetic  36 us (7%)
  blocking collectives  31.4 us (6%)
  local copies, waits for them, and re-layouts  21.8 us (4%)
  matrix products  18.9 us (4%)
  between operations  17 us (3%)
    reduce_scatter x1, waiting for transfers between devices, local(): lax.psum_scatter(jnp.stack([g_up, g_down], axis=1).astype(jnp.bfloat16),...  221 us
    all_gather x1, waiting for transfers between devices, local(): block_rows = lax.all_gather(local_b, 'shard', axis=0, tiled=True)  137 us
    psum x1, blocking collectives, local(): distances = lax.psum(partial_row, 'shard')  31.4 us
    all_gather x1, waiting for transfers between devices, local(): lax.all_gather(score_b[None], 'particle', axis=0, tiled=True)  19.6 us
    slice x1, local copies, waits for them, and re-layouts, local(): block_rows[:, 1, :]  17.1 us
    dot_general x1, matrix products, local(): lax.dot_general(left_cols, up_grad, contract, preferred_element_type=jnp....  11.7 us
  transfers between devices with their start and end apart: 4, of which 3 were waited for; matrix products, arithmetic and copies ran while one was open for 3% of the time, Pallas kernels for 0%

commit v1 on v0

--- a/solution.py
+++ b/solution.py
@@ -22,7 +22,9 @@
     )
     upstream = cotangent[0]
     local_b = weights[0].astype(jnp.bfloat16)
-    block_rows = lax.all_gather(local_b, "shard", axis=0, tiled=True)
+    block_rows = jnp.concatenate(
+        lax.all_to_all(jnp.stack([local_b] * lax.axis_size("shard")), "shard", 0, 0), axis=0
+    )
     left_cols = normed
     right_cols = upstream
     up_part = jnp.dot(left_cols, block_rows[:, 0, :], preferred_element_type=jnp.float32)

time: 504 us -> 570 us (1.13)
  waiting for transfers between devices: 379 us -> 436 us
  starting transfers between devices: 0.35 us -> 12.2 us
  other arithmetic: 36 us -> 27 us
    all_to_all x0 -> x1, waiting for transfers between devices: none -> 190 us  [local(): lax.all_to_all(jnp.stack([local_b] * lax.axis_size('shard')), 'shard', 0, 0)]
    all_gather x1 -> x0, waiting for transfers between devices: 137 us -> none  [local(): block_rows = lax.all_gather(local_b, 'shard', axis=0, tiled=True)]
    slice x1 -> x0, local copies, waits for them, and re-layouts: 17.1 us -> none  [local(): block_rows[:, 1, :]]
    all_to_all x0 -> x1, starting transfers between devices: none -> 11.9 us  [local(): lax.all_to_all(jnp.stack([local_b] * lax.axis_size('shard')), 'shard', 0, 0)]
    all_to_all x0 -> x1, local copies, waits for them, and re-layouts: none -> 8.27 us  [local(): lax.all_to_all(jnp.stack([local_b] * lax.axis_size('shard')), 'shard', 0, 0)]
    unnamed x21 -> x25, local copies, waits for them, and re-layouts: 2.38 us -> 9.11 us
  transfers between devices with their start and end apart: 4 -> 4, of which waited for: 3 -> 3; matrix products, arithmetic and copies ran while one was open for 3% -> 2% of each run, Pallas kernels for 0% -> 0%
where the time goes in v1:
time: 570 us
  waiting for transfers between devices  436 us (76%)
  blocking collectives  31.2 us (5%)
  other arithmetic  27 us (5%)
  local copies, waits for them, and re-layouts  23.8 us (4%)
  matrix products  21.9 us (4%)
  between operations  17 us (3%)
  starting transfers between devices  12.2 us (2%)
    reduce_scatter x1, waiting for transfers between devices, local(): lax.psum_scatter(jnp.stack([g_up, g_down], axis=1).astype(jnp.bfloat16),...  226 us
    all_to_all x1, waiting for transfers between devices, local(): lax.all_to_all(jnp.stack([local_b] * lax.axis_size('shard')), 'shard', 0, 0)  190 us
    psum x1, blocking collectives, local(): distances = lax.psum(partial_row, 'shard')  31.2 us
    all_gather x1, waiting for transfers between devices, local(): lax.all_gather(score_b[None], 'particle', axis=0, tiled=True)  19.7 us
    all_to_all x1, starting transfers between devices, local(): lax.all_to_all(jnp.stack([local_b] * lax.axis_size('shard')), 'shard', 0, 0)  11.9 us
  transfers between devices with their start and end apart: 4, of which 3 were waited for; matrix products, arithmetic and copies ran while one was open for 2% of the time, Pallas kernels for 0%

profile of v1, /device:TPU:1, one launch (start us, length us, event | category | flops | bytes accessed | tf_op | source)
XLA Modules:
  0.0 569.5 jit_solution(3399845852195042042)
XLA Ops:
  8.0 0.0 copy-start
  8.0 1.9 copy.53
  10.0 0.0 copy-start.2
  10.0 4.3 stack.11
  14.3 0.0 copy-done.2
  14.3 0.0 copy-start.8
  14.3 11.9 %all-to-all-start = ((bf16[16,64,2,2048]{3,1,2,0:T(8,128)(2,1)}), bf16[16,64,2,2048]{3,1,2,0:T(8,128)(2,1)}, u32[]{:S(2)}, u32[]{:S(2)}) async-start(bf16[16,64,2,2048]{3,1,2,0:T(8,128)(2,1)} %stack.11), calls=%async_computation | async-start | bytes 16777216 | tf_op jit(solution)/shard_map/all_to_all | solution.py:26
  26.2 0.0 reduce-scatter.2.cloned.1.call-start
  26.3 0.0 copy-done.8
  26.3 0.0 copy-done
  26.3 2.1 gather_fusion
  28.4 0.4 fusion.9
  28.9 190.2 %all-to-all-done = bf16[16,64,2,2048]{3,1,2,0:T(8,128)(2,1)} async-done(((bf16[16,64,2,2048]{3,1,2,0:T(8,128)(2,1)}), bf16[16,64,2,2048]{3,1,2,0:T(8,128)(2,1)}, u32[]{:S(2)}, u32[]{:S(2)}) %all-to-all-start) | async-done | bytes 8388640 | tf_op jit(solution)/shard_map/all_to_all | solution.py:26
  219.1 8.3 %copy.24 = bf16[16,64,2,2048]{3,1,0,2:T(8,128)(2,1)} copy(bf16[16,64,2,2048]{3,1,2,0:T(8,128)(2,1)} %all-to-all-done) | data formatting | bytes 16777216 | tf_op jit(solution)/shard_map/all_to_all | solution.py:26
  227.4 0.0 copy-start.9
  227.4 6.7 %fusion.5 = f32[512,2048]{1,0:T(8,128)} fusion(bf16[1024,2,2048]{2,0,1:T(8,128)(2,1)} %bitcast.58, f32[512]{0:T(512)S(1)} %add_rsqrt_fusion, bf16[512,1024]{1,0:T(8,128)(2,1)S(1)} %gather_fusion, pred[512]{0:T(512)(128)(4,1)S(1)} %compare_and_fusion), kind=kOutput, calls=%fused_computation.13 | convolution fusion | flops 2149580800 | bytes 9439744 | tf_op jit(solution)/shard_map/dot_general | solution.py:30
  234.1 0.0 copy-done.9
  234.1 9.3 %fusion.7 = bf16[1024,1,2048]{2,0,1:T(8,128)(2,1)} fusion(f32[512,2048]{1,0:T(8,128)} %fusion.5, bf16[1024,2,2048]{2,0,1:T(8,128)(2,1)} %bitcast.59, bf16[1,512,1024]{2,1,0:T(8,128)(2,1)S(1)} %copy-done.9, f32[512]{0:T(512)S(1)} %add_rsqrt_fusion, bf16[512,1024]{1,0:T(8,128)(2,1)S(1)} %gather_fusion, pred[512]{0:T(512)(128)(4,1)S(1)} %compare_and_fusion), kind=kOutput, calls=%fused_computation.19 | convolution fusion | flops 4313841664 | bytes 14682624 | tf_op jit(solution)/shard_map/dot_general | solution.py:41
  243.4 0.0 copy-start.5
  243.4 5.9 %fusion.8 = bf16[1024,1,2048]{2,0,1:T(8,128)(2,1)} fusion(f32[512,2048]{1,0:T(8,128)} %fusion.5, bf16[1,512,1024]{2,1,0:T(8,128)(2,1)S(1)} %copy-done.9), kind=kOutput, calls=%fused_computation.20 | convolution fusion | flops 2157969408 | bytes 9437184 | tf_op jit(solution)/shard_map/dot_general | solution.py:42
  249.3 0.0 copy-done.5
  249.3 6.2 %pad_maximum_fusion = bf16[1024,2,2048]{2,0,1:T(8,128)(2,1)} fusion(bf16[1024,1,2048]{2,0,1:T(8,128)(2,1)} %fusion.8, bf16[1024,1,2048]{2,0,1:T(8,128)(2,1)S(1)} %copy-done.5), kind=kLoop, calls=%fused_computation.9 | loop fusion | flops 4194304 | bytes 16777216 | tf_op jit(solution)/shard_map/stack | solution.py:46
  255.4 0.0 copy-start.3
  255.4 0.0 reduce-scatter.2.cloned.1.call-update
  255.5 0.0 all-gather.4.cloned.1.call-start
  255.5 0.5 all-gather.4.cloned.1.call-update
  256.0 0.2 all-gather.6.cloned.1.call-start
  256.3 225.9 %reduce-scatter.2.cloned.1.call-done = bf16[64,2,2048]{2,0,1:T(8,128)(2,1)} async-done(((bf16[1024,2,2048]{2,0,1:T(8,128)(2,1)}), bf16[64,2,2048]{2,0,1:T(8,128)(2,1)}) %reduce-scatter.2.cloned.1.call-update) | async-done | bytes 524304 | tf_op jit(solution)/shard_map/reduce_scatter | solution.py:45
  482.2 1.9 negate_convert_fusion
  484.1 0.0 all-gather.6.cloned.1.call-update
  484.1 0.0 copy-done.3
  484.1 0.1 convert_element_type.45
  484.9 0.0 all-gather.4.cloned.1.call-done
  485.0 5.7 %fusion.1 = f32[16]{0:T(128)S(1)} fusion(bf16[16,64,2,2048]{3,1,2,0:T(8,128)(2,1)} %all-gather.4.cloned.1.call-done, f32[64,2,2048]{2,0,1:T(8,128)S(1)} %convert_element_type.45), kind=kLoop, calls=%fused_computation.4 | loop fusion | flops 16777200 | bytes 9437248 | tf_op jit(solution)/shard_map/reduce_sum | solution.py:61
  490.7 31.2 %psum.7 = f32[16]{0:T(128)S(1)} all-reduce(f32[16]{0:T(128)S(1)} %fusion.1), channel_id=1, replica_groups=mesh['particle'=16,'shard'=16] {'shard'}, use_global_device_ids=true, to_apply=%region_1.2 | all-reduce | flops 16 | bytes 128 | tf_op jit(solution)/shard_map/psum | solution.py:62
  521.9 0.6 fusion.26
  523.2 19.7 %all-gather.6.cloned.1.call-done = bf16[1024,2,2048]{2,0,1:T(8,128)(2,1)} async-done(((bf16[64,2,2048]{2,0,1:T(8,128)(2,1)}), bf16[1024,2,2048]{2,0,1:T(8,128)(2,1)}) %all-gather.6.cloned.1.call-update) | async-done | bytes 8388624 | tf_op jit(solution)/shard_map/all_gather | solution.py:57
  542.9 7.9 %fusion.4 = bf16[16,64,2,2048]{3,1,2,0:T(8,128)(2,1)S(1)} fusion(bf16[16,64,2,2048]{3,1,2,0:T(8,128)(2,1)} %all-gather.4.cloned.1.call-done, f32[]{:T(128)S(6)} %mul_shard_map.3, f32[16]{0:T(128)S(1)} %get-tuple-element.9, bf16[16,64,2,2048]{3,1,0,2:T(8,128)(2,1)} %bitcast.57), kind=kLoop, calls=%fused_computation.7 | loop fusion | flops 25165824 | bytes 25165892 | tf_op jit(solution)/shard_map/convert_element_type | solution.py:66
  550.8 0.0 copy-start.4
  550.8 0.0 copy-start.6
  550.8 0.0 copy-start.7
  550.8 1.9 convert_reduce_fusion
  552.7 0.0 copy-done.4
  552.7 0.0 copy-done.6
  552.7 0.0 copy-done.7
  552.7 2.2 fusion.18
  555.0 0.0 copy-start.1
  555.0 1.8 copy.28
  556.8 1.8 copy.29
  558.5 1.8 copy.30
  560.3 1.8 copy.31
  562.1 0.0 copy-done.1
  (4 shorter events, 0.0 us)
Async XLA Ops:
  8.0 18.3 %copy-start = (bf16[1024,1024]{1,0:T(8,128)(2,1)S(1)}, bf16[1024,1024]{1,0:T(8,128)(2,1)}, u32[]{:S(2)}) copy-start(bf16[1024,1024]{1,0:T(8,128)(2,1)} %param.7) | copy-start | bytes 6291460
  10.0 4.3 copy-start.2
  14.3 12.0 %copy-start.8 = (s32[512]{0:T(512)S(1)}, s32[512]{0:T(512)}, u32[]{:S(2)}) copy-start(s32[512]{0:T(512)} %param.8) | copy-start | bytes 6148
  14.3 204.8 %all-to-all-start = ((bf16[16,64,2,2048]{3,1,2,0:T(8,128)(2,1)}), bf16[16,64,2,2048]{3,1,2,0:T(8,128)(2,1)}, u32[]{:S(2)}, u32[]{:S(2)}) async-start(bf16[16,64,2,2048]{3,1,2,0:T(8,128)(2,1)} %stack.11), calls=%async_computation | async-start | bytes 16777216 | tf_op jit(solution)/shard_map/all_to_all | solution.py:26
  26.2 455.9 %reduce-scatter.2.cloned.1.call-start = ((), (), s32[]{:S(2)}) async-start(), calls=%async_computation.3 | async-start | bytes 8912896 | tf_op jit(solution)/shard_map/reduce_scatter | solution.py:45
  227.4 6.7 %copy-start.9 = (bf16[1,512,1024]{2,1,0:T(8,128)(2,1)S(1)}, bf16[1,512,1024]{2,1,0:T(8,128)(2,1)}, u32[]{:S(2)}) copy-start(bf16[1,512,1024]{2,1,0:T(8,128)(2,1)} %param.10) | copy-start | bytes 3145732
  243.4 5.9 %copy-start.5 = (bf16[1024,1,2048]{2,0,1:T(8,128)(2,1)S(1)}, bf16[1024,1,2048]{2,0,1:T(8,128)(2,1)}, u32[]{:S(2)}) copy-start(bf16[1024,1,2048]{2,0,1:T(8,128)(2,1)} %fusion.7) | copy-start | bytes 12582916
  255.4 228.7 %copy-start.3 = (bf16[1,64,2,2048]{3,1,2,0:T(8,128)(2,1)S(1)}, bf16[1,64,2,2048]{3,1,2,0:T(8,128)(2,1)}, u32[]{:S(2)}) copy-start(bf16[1,64,2,2048]{3,1,2,0:T(8,128)(2,1)} %copy-done.2) | copy-start | bytes 1572868
  255.5 229.5 %all-gather.4.cloned.1.call-start = ((), (), s32[]{:S(2)}) async-start(), calls=%async_computation.2 | async-start | bytes 8912896 | tf_op jit(solution)/shard_map/all_gather | solution.py:56
  256.0 286.9 %all-gather.6.cloned.1.call-start = ((), (), s32[]{:S(2)}) async-start(), calls=%async_computation.4 | async-start | bytes 8912896 | tf_op jit(solution)/shard_map/all_gather | solution.py:57
  550.8 1.9 copy-start.4
  550.8 1.9 copy-start.6
  550.8 1.9 copy-start.7
  555.0 7.1 %copy-start.1 = (bf16[1024,1024]{1,0:T(8,128)(2,1)S(1)}, bf16[1024,1024]{1,0:T(8,128)(2,1)}, u32[]{:S(2)}) copy-start(bf16[1024,1024]{1,0:T(8,128)(2,1)} %param.7) | copy-start | bytes 6291460
Sparse Core Ops, SparseCore 0:
  255.6 226.5 reduce-scatter.1
Sparse Core Ops, SparseCore 1:
  258.4 63.2 all-gather.3
  484.2 58.6 all-gather.5
